TPU v7x, 256 devices: a whole 4x4x8 slice. The times are simulated.
256 devices in a mesh: pairs: 32 (over y, z), tm: 8 (over x, core).
Axes of the slice: x: 4, y: 4, z: 8, core: 2. Of those that a mesh axis runs over, the one named last changes fastest.
Arguments:
- spectra: bfloat16 [8, 256, 2, 32768], P('tm', 'pairs'), may hold values from -6 to 6
- channel_slot: int32 [256], P('pairs'), may hold values from 0 to 7, as said below
- tile_list: int32 [63, 2], replicated, may hold values from 0 to 31, as said below
- tile_owner: int32 [63], replicated, may hold values from 0 to 31, as said below
Outputs:
- correlations: float32 [128, 64, 256], P('pairs', 'tm')
Inputs may be any that keep to these rules, and one draw needn't show every extreme that they name: `channel_slot`: within each block of 8 channels the values are a permutation of 0..7. `tile_list`: each row (i, j) has j = i or j = i + 1; every such pair of blocks appears exactly once, in some order. `tile_owner`: the owner of the tile in row p of tile_list is that row's i or i + 1; the tile of blocks 0 and 1 is owned by block 1; no owner holds more than 4 tiles, and some owner holds exactly 4.
All inputs are finite; a program needn't handle non-finite values.
Results may differ from a plain program's by a relative error of at most 0.00033.
Values may be sent and summed in bfloat16 or wider, within the bound.
A program may use at most 64 MiB of HBM per device.

v0:
```python
import math
import jax
import jax.numpy as jnp
from jax import lax
from jax.sharding import PartitionSpec as P

LAGS = 256
TILE_CAP = 4


def extended(block, sides, width):
    for axis, dim in sides:
        count = lax.axis_size(axis)
        forward = [(i, i + 1) for i in range(count - 1)]
        backward = [(target, source) for source, target in forward]
        low = lax.ppermute(
            lax.slice_in_dim(block, block.shape[dim] - width, None, axis=dim), axis, forward
        )
        high = lax.ppermute(lax.slice_in_dim(block, 0, width, axis=dim), axis, backward)
        block = jnp.concatenate([low, block, high], axis=dim)
    return block


def lag_table(freq_start, freq_width, bin_count, lag_count):
    freq_ids = freq_start + lax.iota(jnp.int32, freq_width)
    shift_lag = lax.iota(jnp.int32, lag_count) - lag_count // 2
    phase_steps = jnp.mod(freq_ids[:, None] * shift_lag[None, :], 2 * bin_count)
    phase_angle = phase_steps.astype(jnp.float32) * (math.pi / bin_count)
    cosine = jnp.cos(phase_angle).astype(jnp.bfloat16)
    sine_neg = (-jnp.sin(phase_angle)).astype(jnp.bfloat16)
    return jnp.concatenate([cosine, sine_neg], axis=0)


def cross_block(lead_block, tail_block):
    group_count = lead_block.shape[0]
    chan_count = lead_block.shape[1]
    lead_real = lead_block[:, :, 0].astype(jnp.float32)[:, :, None, :]
    lead_imag = lead_block[:, :, 1].astype(jnp.float32)[:, :, None, :]
    tail_real = tail_block[:, :, 0].astype(jnp.float32)[:, None, :, :]
    tail_imag = tail_block[:, :, 1].astype(jnp.float32)[:, None, :, :]
    real_part = lead_real * tail_real + lead_imag * tail_imag
    imag_part = lead_imag * tail_real - lead_real * tail_imag
    joined = jnp.concatenate(
        [real_part.astype(jnp.bfloat16), imag_part.astype(jnp.bfloat16)], axis=-1
    )
    return joined.reshape(group_count, chan_count * chan_count, joined.shape[-1])


def correlate(blocks, lead_pos, tail_pos, norm_scale):
    chan_count = blocks.shape[1]
    bin_count = blocks.shape[3]
    freq_width = min(2048, bin_count)
    slot_count = lead_pos.shape[0]

    def freq_turn(step_index, running):
        freq_start = step_index * freq_width
        freq_piece = lax.dynamic_slice_in_dim(blocks, freq_start, freq_width, 3)
        lead_block = jnp.take(freq_piece, lead_pos, axis=0)
        tail_block = jnp.take(freq_piece, tail_pos, axis=0)
        cross_spec = cross_block(lead_block, tail_block)
        lag_rows = lag_table(freq_start, freq_width, bin_count, LAGS)
        return running + jnp.einsum(
            "spf,fl->spl", cross_spec, lag_rows, preferred_element_type=jnp.float32
        )

    start_sum = jnp.zeros((slot_count, chan_count * chan_count, LAGS), jnp.float32)
    running = lax.fori_loop(0, bin_count // freq_width, freq_turn, start_sum)
    return running * norm_scale


def stack_windows(window_terms):
    summed = lax.psum(window_terms, "tm")
    share_rows = summed.shape[1] // lax.axis_size("tm")
    return lax.dynamic_slice_in_dim(summed, lax.axis_index("tm") * share_rows, share_rows, 1)


def on_device(spectra, channel_slot, tile_list, tile_owner):
    here_index = lax.axis_index("pairs")
    bin_count = spectra.shape[3]
    norm_scale = 1.0 / math.sqrt(2.0 * bin_count * lax.axis_size("tm"))
    ordered = jnp.take(spectra[0], channel_slot, axis=0)
    chan_count = ordered.shape[0]
    tile_count = tile_list.shape[0]
    low_block = tile_list[:, 0]
    high_block = tile_list[:, 1]
    earlier = lax.iota(jnp.int32, tile_count)[:, None] > lax.iota(jnp.int32, tile_count)[None, :]
    slot_rank = jnp.sum((tile_owner[:, None] == tile_owner[None, :]) & earlier, axis=1)
    slot_ids = lax.iota(jnp.int32, TILE_CAP)
    owned_slot = (
        (tile_owner[None, :] == here_index) & (slot_rank[None, :] == slot_ids[:, None])
    ).astype(jnp.int32)
    live_slot = jnp.sum(owned_slot, axis=1)
    slot_low = jnp.sum(owned_slot * low_block[None, :], axis=1)
    slot_high = jnp.sum(owned_slot * high_block[None, :], axis=1)
    widened = extended(ordered, (("pairs", 0),), chan_count)
    blocks = widened.reshape(3, chan_count, widened.shape[1], widened.shape[2])
    lead_pos = jnp.clip(slot_low - here_index + 1, 0, 2)
    tail_pos = jnp.clip(slot_high - here_index + 1, 0, 2)
    window_terms = correlate(blocks, lead_pos, tail_pos, norm_scale)
    window_terms = window_terms * live_slot[:, None, None].astype(jnp.float32)
    return stack_windows(window_terms)


def solution(mesh):
    placed = (P("tm", "pairs", None, None), P("pairs"), P(), P())
    return jax.shard_map(
        on_device, mesh=mesh, in_specs=placed, out_specs=P("pairs", "tm", None), check_vma=False
    )
```

profile of v0, /device:TPU:8, one launch (start us, length us, event | category | flops | bytes accessed | tf_op | source)
XLA Modules:
  0.0 379.8 jit_solution(1595996826397353993)
XLA Ops:
  8.0 2.7 gather_fusion.2
  11.6 7.7 %collective-permute-start.1 = (bf16[8,2,32768]{2,1,0:T(2,128)(2,1)S(1)}, bf16[8,2,32768]{2,1,0:T(2,128)(2,1)S(1)}, u32[]{:S(2)}, u32[]{:S(2)}) collective-permute-start(bf16[8,2,32768]{2,1,0:T(2,128)(2,1)S(1)} %broadcast_select_fusion.2), channel_id=1, source_target_pairs={{8,0},{16,8},{24,16},{32,24},{40,32},{48,40},{56,48},{64,56},{72,6... | collective-permute-start | bytes 3145736 | tf_op jit(solution)/shard_map/ppermute | solution.py:19
  19.3 1.9 collective-permute-start
  21.6 20.1 %collective-permute-done.1 = bf16[8,2,32768]{2,1,0:T(2,128)(2,1)S(1)} collective-permute-done((bf16[8,2,32768]{2,1,0:T(2,128)(2,1)S(1)}, bf16[8,2,32768]{2,1,0:T(2,128)(2,1)S(1)}, u32[]{:S(2)}, u32[]{:S(2)}) %collective-permute-start.1) | collective-permute-done | bytes 1048608 | tf_op jit(solution)/shard_map/ppermute | solution.py:19
  41.7 6.3 %collective-permute-done = bf16[8,2,32768]{2,1,0:T(2,128)(2,1)} collective-permute-done((bf16[8,2,32768]{2,1,0:T(2,128)(2,1)S(1)}, bf16[8,2,32768]{2,1,0:T(2,128)(2,1)}, u32[]{:S(2)}, u32[]{:S(2)}) %collective-permute-start) | collective-permute-done | bytes 1048608 | tf_op jit(solution)/shard_map/ppermute | solution.py:16
  48.0 7.1 %pad_maximum_fusion = bf16[24,2,32768]{2,1,0:T(2,128)(2,1)} fusion(bf16[8,2,32768]{2,1,0:T(2,128)(2,1)S(1)} %collective-permute-done.1, bf16[8,2,32768]{2,1,0:T(2,128)(2,1)S(1)} %broadcast_select_fusion.2, bf16[8,2,32768]{2,1,0:T(2,128)(2,1)} %collective-permute-done), kind=kLoop, calls=%fused_computation.45 | loop fusion | flops 3145728 | bytes 6291456 | tf_op jit(solution)/shard_map/concatenate | solution.py:20
  55.1 254.1 %while.16 = (s32[]{:T(128)}, f32[4,64,256]{2,1,0:T(8,128)S(1)}, bf16[3,8,2,32768]{3,2,1,0:T(2,128)(2,1)}, s32[4]{0:T(128)S(1)}, s32[4]{0:T(128)S(1)}, /*index=5*/s32[]{:T(128)}, s32[]{:T(128)}, s32[]{:T(128)}, s32[]{:T(128)}) while((s32[]{:T(128)}, f32[4,64,256]{2,1,0:T(8,128)S(1)}, bf16[3,8,2,32768]{3,2,1,0:T(2,128)(2,1)}, ...), condition=%wide.region_4.6_spmd.clone, body=%wide.region_3.5_spmd.clone.sunk | while | flops 559026496 | bytes 16148821 | solution.py:67
  56.3 1.1 gather_fusion.1
  57.7 1.1 gather_fusion
  60.7 9.4 %cosine_convert_fusion.2 = (bf16[2048,256]{1,0:T(8,128)(2,1)S(1)}, bf16[2048,256]{1,0:T(8,128)(2,1)S(1)}) fusion(s32[256]{0:T(256)S(1)} %iota_add_fusion.4, s32[2048]{0:T(1024)S(1)} %iota_add_fusion.5), kind=kLoop, calls=%fused_computation.19.clone.1 | loop fusion | flops 8912896 | bytes 2106368 | tf_op jit(solution)/shard_map/while/body/eval_jaxpr/convert_element_type | solution.py:29
  72.2 1.1 gather_fusion.1
  73.5 1.1 gather_fusion
  76.6 9.4 %cosine_convert_fusion.2 = (bf16[2048,256]{1,0:T(8,128)(2,1)S(1)}, bf16[2048,256]{1,0:T(8,128)(2,1)S(1)}) fusion(s32[256]{0:T(256)S(1)} %iota_add_fusion.4, s32[2048]{0:T(1024)S(1)} %iota_add_fusion.5), kind=kLoop, calls=%fused_computation.19.clone.1 | loop fusion | flops 8912896 | bytes 2106368 | tf_op jit(solution)/shard_map/while/body/eval_jaxpr/convert_element_type | solution.py:29
  88.0 1.1 gather_fusion.1
  89.4 1.1 gather_fusion
  92.5 9.4 %cosine_convert_fusion.2 = (bf16[2048,256]{1,0:T(8,128)(2,1)S(1)}, bf16[2048,256]{1,0:T(8,128)(2,1)S(1)}) fusion(s32[256]{0:T(256)S(1)} %iota_add_fusion.4, s32[2048]{0:T(1024)S(1)} %iota_add_fusion.5), kind=kLoop, calls=%fused_computation.19.clone.1 | loop fusion | flops 8912896 | bytes 2106368 | tf_op jit(solution)/shard_map/while/body/eval_jaxpr/convert_element_type | solution.py:29
  103.9 1.1 gather_fusion.1
  105.3 1.1 gather_fusion
  108.4 9.4 %cosine_convert_fusion.2 = (bf16[2048,256]{1,0:T(8,128)(2,1)S(1)}, bf16[2048,256]{1,0:T(8,128)(2,1)S(1)}) fusion(s32[256]{0:T(256)S(1)} %iota_add_fusion.4, s32[2048]{0:T(1024)S(1)} %iota_add_fusion.5), kind=kLoop, calls=%fused_computation.19.clone.1 | loop fusion | flops 8912896 | bytes 2106368 | tf_op jit(solution)/shard_map/while/body/eval_jaxpr/convert_element_type | solution.py:29
  119.8 1.1 gather_fusion.1
  121.2 1.1 gather_fusion
  124.2 9.4 %cosine_convert_fusion.2 = (bf16[2048,256]{1,0:T(8,128)(2,1)S(1)}, bf16[2048,256]{1,0:T(8,128)(2,1)S(1)}) fusion(s32[256]{0:T(256)S(1)} %iota_add_fusion.4, s32[2048]{0:T(1024)S(1)} %iota_add_fusion.5), kind=kLoop, calls=%fused_computation.19.clone.1 | loop fusion | flops 8912896 | bytes 2106368 | tf_op jit(solution)/shard_map/while/body/eval_jaxpr/convert_element_type | solution.py:29
  135.7 1.1 gather_fusion.1
  137.1 1.1 gather_fusion
  140.1 9.4 %cosine_convert_fusion.2 = (bf16[2048,256]{1,0:T(8,128)(2,1)S(1)}, bf16[2048,256]{1,0:T(8,128)(2,1)S(1)}) fusion(s32[256]{0:T(256)S(1)} %iota_add_fusion.4, s32[2048]{0:T(1024)S(1)} %iota_add_fusion.5), kind=kLoop, calls=%fused_computation.19.clone.1 | loop fusion | flops 8912896 | bytes 2106368 | tf_op jit(solution)/shard_map/while/body/eval_jaxpr/convert_element_type | solution.py:29
  151.6 1.1 gather_fusion.1
  152.9 1.1 gather_fusion
  156.0 9.4 %cosine_convert_fusion.2 = (bf16[2048,256]{1,0:T(8,128)(2,1)S(1)}, bf16[2048,256]{1,0:T(8,128)(2,1)S(1)}) fusion(s32[256]{0:T(256)S(1)} %iota_add_fusion.4, s32[2048]{0:T(1024)S(1)} %iota_add_fusion.5), kind=kLoop, calls=%fused_computation.19.clone.1 | loop fusion | flops 8912896 | bytes 2106368 | tf_op jit(solution)/shard_map/while/body/eval_jaxpr/convert_element_type | solution.py:29
  167.4 1.1 gather_fusion.1
  168.8 1.1 gather_fusion
  171.9 9.4 %cosine_convert_fusion.2 = (bf16[2048,256]{1,0:T(8,128)(2,1)S(1)}, bf16[2048,256]{1,0:T(8,128)(2,1)S(1)}) fusion(s32[256]{0:T(256)S(1)} %iota_add_fusion.4, s32[2048]{0:T(1024)S(1)} %iota_add_fusion.5), kind=kLoop, calls=%fused_computation.19.clone.1 | loop fusion | flops 8912896 | bytes 2106368 | tf_op jit(solution)/shard_map/while/body/eval_jaxpr/convert_element_type | solution.py:29
  183.3 1.1 gather_fusion.1
  184.7 1.1 gather_fusion
  187.8 9.4 %cosine_convert_fusion.2 = (bf16[2048,256]{1,0:T(8,128)(2,1)S(1)}, bf16[2048,256]{1,0:T(8,128)(2,1)S(1)}) fusion(s32[256]{0:T(256)S(1)} %iota_add_fusion.4, s32[2048]{0:T(1024)S(1)} %iota_add_fusion.5), kind=kLoop, calls=%fused_computation.19.clone.1 | loop fusion | flops 8912896 | bytes 2106368 | tf_op jit(solution)/shard_map/while/body/eval_jaxpr/convert_element_type | solution.py:29
  199.2 1.1 gather_fusion.1
  200.6 1.1 gather_fusion
  203.7 9.4 %cosine_convert_fusion.2 = (bf16[2048,256]{1,0:T(8,128)(2,1)S(1)}, bf16[2048,256]{1,0:T(8,128)(2,1)S(1)}) fusion(s32[256]{0:T(256)S(1)} %iota_add_fusion.4, s32[2048]{0:T(1024)S(1)} %iota_add_fusion.5), kind=kLoop, calls=%fused_computation.19.clone.1 | loop fusion | flops 8912896 | bytes 2106368 | tf_op jit(solution)/shard_map/while/body/eval_jaxpr/convert_element_type | solution.py:29
  215.1 1.1 gather_fusion.1
  219.5 9.4 %cosine_convert_fusion.2 = (bf16[2048,256]{1,0:T(8,128)(2,1)S(1)}, bf16[2048,256]{1,0:T(8,128)(2,1)S(1)}) fusion(s32[256]{0:T(256)S(1)} %iota_add_fusion.4, s32[2048]{0:T(1024)S(1)} %iota_add_fusion.5), kind=kLoop, calls=%fused_computation.19.clone.1 | loop fusion | flops 8912896 | bytes 2106368 | tf_op jit(solution)/shard_map/while/body/eval_jaxpr/convert_element_type | solution.py:29
  235.4 9.4 %cosine_convert_fusion.2 = (bf16[2048,256]{1,0:T(8,128)(2,1)S(1)}, bf16[2048,256]{1,0:T(8,128)(2,1)S(1)}) fusion(s32[256]{0:T(256)S(1)} %iota_add_fusion.4, s32[2048]{0:T(1024)S(1)} %iota_add_fusion.5), kind=kLoop, calls=%fused_computation.19.clone.1 | loop fusion | flops 8912896 | bytes 2106368 | tf_op jit(solution)/shard_map/while/body/eval_jaxpr/convert_element_type | solution.py:29
  251.3 9.4 %cosine_convert_fusion.2 = (bf16[2048,256]{1,0:T(8,128)(2,1)S(1)}, bf16[2048,256]{1,0:T(8,128)(2,1)S(1)}) fusion(s32[256]{0:T(256)S(1)} %iota_add_fusion.4, s32[2048]{0:T(1024)S(1)} %iota_add_fusion.5), kind=kLoop, calls=%fused_computation.19.clone.1 | loop fusion | flops 8912896 | bytes 2106368 | tf_op jit(solution)/shard_map/while/body/eval_jaxpr/convert_element_type | solution.py:29
  267.2 9.4 %cosine_convert_fusion.2 = (bf16[2048,256]{1,0:T(8,128)(2,1)S(1)}, bf16[2048,256]{1,0:T(8,128)(2,1)S(1)}) fusion(s32[256]{0:T(256)S(1)} %iota_add_fusion.4, s32[2048]{0:T(1024)S(1)} %iota_add_fusion.5), kind=kLoop, calls=%fused_computation.19.clone.1 | loop fusion | flops 8912896 | bytes 2106368 | tf_op jit(solution)/shard_map/while/body/eval_jaxpr/convert_element_type | solution.py:29
  280.0 1.1 gather_fusion
  283.1 9.4 %cosine_convert_fusion.2 = (bf16[2048,256]{1,0:T(8,128)(2,1)S(1)}, bf16[2048,256]{1,0:T(8,128)(2,1)S(1)}) fusion(s32[256]{0:T(256)S(1)} %iota_add_fusion.4, s32[2048]{0:T(1024)S(1)} %iota_add_fusion.5), kind=kLoop, calls=%fused_computation.19.clone.1 | loop fusion | flops 8912896 | bytes 2106368 | tf_op jit(solution)/shard_map/while/body/eval_jaxpr/convert_element_type | solution.py:29
  295.9 1.1 gather_fusion
  299.0 9.4 %cosine_convert_fusion.2 = (bf16[2048,256]{1,0:T(8,128)(2,1)S(1)}, bf16[2048,256]{1,0:T(8,128)(2,1)S(1)}) fusion(s32[256]{0:T(256)S(1)} %iota_add_fusion.4, s32[2048]{0:T(1024)S(1)} %iota_add_fusion.5), kind=kLoop, calls=%fused_computation.19.clone.1 | loop fusion | flops 8912896 | bytes 2106368 | tf_op jit(solution)/shard_map/while/body/eval_jaxpr/convert_element_type | solution.py:29
  310.0 61.6 %all-reduce.2.cloned.1.call-done = f32[4,64,256]{2,1,0:T(8,128)} async-done(((f32[4,64,256]{2,1,0:T(8,128)}), f32[4,64,256]{2,1,0:T(8,128)}) %all-reduce.2.cloned.1.call-update) | async-done | bytes 262160 | tf_op jit(solution)/shard_map/psum | solution.py:72
  371.6 1.4 constant_dynamic-slice_fusion.1
  (301 shorter events, 79.5 us)
Async XLA Ops:
  6.5 1.4 copy-start
  6.5 365.1 %all-reduce.2.cloned.1.call-start = ((), (), s32[]{:S(2)}) async-start(), calls=%async_computation | async-start | bytes 524288 | tf_op jit(solution)/shard_map/psum | solution.py:72
  8.0 13.3 %copy-start.2 = (s32[63]{0:T(128)S(1)}, s32[63]{0:T(128)}, u32[]{:S(2)}) copy-start(s32[63]{0:T(128)} %param.11) | copy-start | bytes 760
  8.0 13.5 %copy-start.1 = (s32[63,2]{0,1:T(2,128)S(1)}, s32[63,2]{0,1:T(2,128)}, u32[]{:S(2)}) copy-start(s32[63,2]{0,1:T(2,128)} %param.10) | copy-start | bytes 1516
  11.6 30.1 %collective-permute-start.1 = (bf16[8,2,32768]{2,1,0:T(2,128)(2,1)S(1)}, bf16[8,2,32768]{2,1,0:T(2,128)(2,1)S(1)}, u32[]{:S(2)}, u32[]{:S(2)}) collective-permute-start(bf16[8,2,32768]{2,1,0:T(2,128)(2,1)S(1)} %broadcast_select_fusion.2), channel_id=1, source_target_pairs={{8,0},{16,8},{24,16},{32,24},{40,32},{48,40},{56,48},{64,56},{72,6... | collective-permute-start | bytes 3145736 | tf_op jit(solution)/shard_map/ppermute | solution.py:19
  19.3 28.7 %collective-permute-start = (bf16[8,2,32768]{2,1,0:T(2,128)(2,1)S(1)}, bf16[8,2,32768]{2,1,0:T(2,128)(2,1)}, u32[]{:S(2)}, u32[]{:S(2)}) collective-permute-start(bf16[8,2,32768]{2,1,0:T(2,128)(2,1)S(1)} %broadcast_select_fusion.2), channel_id=1, source_target_pairs={{0,8},{8,16},{16,24},{24,32},{32,40},{40,48},{48,56},{56,64},{64,7... | collective-permute-start | bytes 3145736 | tf_op jit(solution)/shard_map/ppermute | solution.py:16
Sparse Core Ops, SparseCore 0:
  310.1 61.4 all-reduce.1
where the time goes:
time: 381 us; the launch traced here: 380 us
  other arithmetic  192 us (50%)
  waiting for transfers between devices  88 us (23%)
  local copies, waits for them, and re-layouts  60.9 us (16%)
  between operations  13.5 us (4%)
  matrix products  12.9 us (3%)
  starting transfers between devices  9.57 us (3%)
    convert_element_type x16, other arithmetic, lag_table(): cosine = jnp.cos(phase_angle).astype(jnp.bfloat16)  151 us
    psum x1, waiting for transfers between devices, stack_windows(): summed = lax.psum(window_terms, 'tm')  61.6 us
    ppermute x1, waiting for transfers between devices, extended(): lax.ppermute(lax.slice_in_dim(block, 0, width, axis=dim), axis, backward)  20.1 us
    gather x16, local copies, waits for them, and re-layouts, freq_turn(): tail_block = jnp.take(freq_piece, tail_pos, axis=0)  17.2 us
    gather x16, local copies, waits for them, and re-layouts, freq_turn(): lead_block = jnp.take(freq_piece, lead_pos, axis=0)  17.2 us
    dynamic_slice x16, local copies, waits for them, and re-layouts, freq_turn(): freq_piece = lax.dynamic_slice_in_dim(blocks, freq_start, freq_width, 3)  17.1 us
    dot_general x16, matrix products, freq_turn(): jnp.einsum('spf,fl->spl', cross_spec, lag_rows, preferred_element_type=jn...  12.9 us
    convert_element_type x16, other arithmetic, cross_block(): real_part.astype(jnp.bfloat16)  8.57 us
  transfers between devices with their start and end apart: 3, of which 3 were waited for; matrix products, arithmetic and copies ran while one was open for 0% of the time, Pallas kernels for 0%

commit v1 on v0

--- a/solution.py
+++ b/solution.py
@@ -1,3 +1,4 @@
+import functools
 import math
 import jax
 import jax.numpy as jnp
@@ -6,6 +7,13 @@
 
 LAGS = 256
 TILE_CAP = 4
+
+
+def attach_the_pieces_all(array_in, along_axis):
+    return jnp.sum(lax.all_gather(array_in, along_axis), axis=0)
+
+
+write_unit_on_mesh = functools.partial(attach_the_pieces_all, along_axis="tm")
 
 
 def extended(block, sides, width):
@@ -69,7 +77,7 @@
 
 
 def stack_windows(window_terms):
-    summed = lax.psum(window_terms, "tm")
+    summed = write_unit_on_mesh(window_terms)
     share_rows = summed.shape[1] // lax.axis_size("tm")
     return lax.dynamic_slice_in_dim(summed, lax.axis_index("tm") * share_rows, share_rows, 1)
 

time: 381 us -> 346 us (0.908)
  waiting for transfers between devices: 88 us -> 50.8 us
    psum x1 -> x0, waiting for transfers between devices: 61.6 us -> none  [stack_windows(): summed = lax.psum(window_terms, 'tm')]
    all_gather x0 -> x1, waiting for transfers between devices: none -> 24.4 us  [attach_the_pieces_all(): return jnp.sum(lax.all_gather(array_in, along_axis), axis=0)]
where the time goes in v1:
time: 346 us; the launch traced here: 344 us
  other arithmetic  195 us (56%)
  local copies, waits for them, and re-layouts  60.2 us (17%)
  waiting for transfers between devices  50.8 us (15%)
  between operations  13.5 us (4%)
  matrix products  13 us (4%)
  starting transfers between devices  9.57 us (3%)
    convert_element_type x16, other arithmetic, lag_table(): cosine = jnp.cos(phase_angle).astype(jnp.bfloat16)  151 us
    all_gather x1, waiting for transfers between devices, attach_the_pieces_all(): return jnp.sum(lax.all_gather(array_in, along_axis), axis=0)  24.4 us
    ppermute x1, waiting for transfers between devices, extended(): lax.ppermute(lax.slice_in_dim(block, 0, width, axis=dim), axis, backward)  20.1 us
    gather x16, local copies, waits for them, and re-layouts, freq_turn(): lead_block = jnp.take(freq_piece, lead_pos, axis=0)  17.2 us
    gather x16, local copies, waits for them, and re-layouts, freq_turn(): tail_block = jnp.take(freq_piece, tail_pos, axis=0)  17.2 us
    dynamic_slice x16, local copies, waits for them, and re-layouts, freq_turn(): freq_piece = lax.dynamic_slice_in_dim(blocks, freq_start, freq_width, 3)  17.1 us
    dot_general x16, matrix products, freq_turn(): jnp.einsum('spf,fl->spl', cross_spec, lag_rows, preferred_element_type=jn...  13 us
    convert_element_type x16, other arithmetic, cross_block(): real_part.astype(jnp.bfloat16)  8.99 us
  transfers between devices with their start and end apart: 3, of which 3 were waited for; matrix products, arithmetic and copies ran while one was open for 0% of the time, Pallas kernels for 0%

profile of v1, /device:TPU:8, one launch (start us, length us, event | category | flops | bytes accessed | tf_op | source)
XLA Modules:
  0.0 344.0 jit_solution(2438151875269254930)
XLA Ops:
  8.0 2.7 gather_fusion.2
  11.6 7.7 %collective-permute-start.1 = (bf16[8,2,32768]{2,1,0:T(2,128)(2,1)S(1)}, bf16[8,2,32768]{2,1,0:T(2,128)(2,1)S(1)}, u32[]{:S(2)}, u32[]{:S(2)}) collective-permute-start(bf16[8,2,32768]{2,1,0:T(2,128)(2,1)S(1)} %broadcast_select_fusion.2), channel_id=1, source_target_pairs={{8,0},{16,8},{24,16},{32,24},{40,32},{48,40},{56,48},{64,56},{72,6... | collective-permute-start | bytes 3145736 | tf_op jit(solution)/shard_map/ppermute | solution.py:27
  19.3 1.9 collective-permute-start
  21.6 20.1 %collective-permute-done.1 = bf16[8,2,32768]{2,1,0:T(2,128)(2,1)S(1)} collective-permute-done((bf16[8,2,32768]{2,1,0:T(2,128)(2,1)S(1)}, bf16[8,2,32768]{2,1,0:T(2,128)(2,1)S(1)}, u32[]{:S(2)}, u32[]{:S(2)}) %collective-permute-start.1) | collective-permute-done | bytes 1048608 | tf_op jit(solution)/shard_map/ppermute | solution.py:27
  41.7 6.3 %collective-permute-done = bf16[8,2,32768]{2,1,0:T(2,128)(2,1)} collective-permute-done((bf16[8,2,32768]{2,1,0:T(2,128)(2,1)S(1)}, bf16[8,2,32768]{2,1,0:T(2,128)(2,1)}, u32[]{:S(2)}, u32[]{:S(2)}) %collective-permute-start) | collective-permute-done | bytes 1048608 | tf_op jit(solution)/shard_map/ppermute | solution.py:24
  48.0 7.1 %pad_maximum_fusion = bf16[24,2,32768]{2,1,0:T(2,128)(2,1)} fusion(bf16[8,2,32768]{2,1,0:T(2,128)(2,1)S(1)} %collective-permute-done.1, bf16[8,2,32768]{2,1,0:T(2,128)(2,1)S(1)} %broadcast_select_fusion.2, bf16[8,2,32768]{2,1,0:T(2,128)(2,1)} %collective-permute-done), kind=kLoop, calls=%fused_computation.45 | loop fusion | flops 3145728 | bytes 6291456 | tf_op jit(solution)/shard_map/concatenate | solution.py:28
  55.1 254.5 %while.16 = (s32[]{:T(128)}, f32[4,64,256]{2,1,0:T(8,128)S(1)}, bf16[3,8,2,32768]{3,2,1,0:T(2,128)(2,1)}, s32[4]{0:T(128)S(1)}, s32[4]{0:T(128)S(1)}, /*index=5*/s32[]{:T(128)}, s32[]{:T(128)}, s32[]{:T(128)}, s32[]{:T(128)}) while((s32[]{:T(128)}, f32[4,64,256]{2,1,0:T(8,128)S(1)}, bf16[3,8,2,32768]{3,2,1,0:T(2,128)(2,1)}, ...), condition=%wide.region_4.6_spmd.clone, body=%wide.region_3.5_spmd.clone.sunk | while | flops 559026496 | bytes 16148821 | solution.py:75
  56.3 1.1 gather_fusion.1
  57.7 1.1 gather_fusion
  60.7 9.4 %cosine_convert_fusion.2 = (bf16[2048,256]{1,0:T(8,128)(2,1)S(1)}, bf16[2048,256]{1,0:T(8,128)(2,1)S(1)}) fusion(s32[256]{0:T(256)S(1)} %iota_add_fusion.4, s32[2048]{0:T(1024)S(1)} %iota_add_fusion.5), kind=kLoop, calls=%fused_computation.19.clone.1 | loop fusion | flops 8912896 | bytes 2106368 | tf_op jit(solution)/shard_map/while/body/eval_jaxpr/convert_element_type | solution.py:37
  72.2 1.1 gather_fusion.1
  73.6 1.1 gather_fusion
  76.7 9.4 %cosine_convert_fusion.2 = (bf16[2048,256]{1,0:T(8,128)(2,1)S(1)}, bf16[2048,256]{1,0:T(8,128)(2,1)S(1)}) fusion(s32[256]{0:T(256)S(1)} %iota_add_fusion.4, s32[2048]{0:T(1024)S(1)} %iota_add_fusion.5), kind=kLoop, calls=%fused_computation.19.clone.1 | loop fusion | flops 8912896 | bytes 2106368 | tf_op jit(solution)/shard_map/while/body/eval_jaxpr/convert_element_type | solution.py:37
  88.1 1.1 gather_fusion.1
  89.5 1.1 gather_fusion
  92.6 9.4 %cosine_convert_fusion.2 = (bf16[2048,256]{1,0:T(8,128)(2,1)S(1)}, bf16[2048,256]{1,0:T(8,128)(2,1)S(1)}) fusion(s32[256]{0:T(256)S(1)} %iota_add_fusion.4, s32[2048]{0:T(1024)S(1)} %iota_add_fusion.5), kind=kLoop, calls=%fused_computation.19.clone.1 | loop fusion | flops 8912896 | bytes 2106368 | tf_op jit(solution)/shard_map/while/body/eval_jaxpr/convert_element_type | solution.py:37
  104.0 1.1 gather_fusion.1
  105.4 1.1 gather_fusion
  108.5 9.4 %cosine_convert_fusion.2 = (bf16[2048,256]{1,0:T(8,128)(2,1)S(1)}, bf16[2048,256]{1,0:T(8,128)(2,1)S(1)}) fusion(s32[256]{0:T(256)S(1)} %iota_add_fusion.4, s32[2048]{0:T(1024)S(1)} %iota_add_fusion.5), kind=kLoop, calls=%fused_computation.19.clone.1 | loop fusion | flops 8912896 | bytes 2106368 | tf_op jit(solution)/shard_map/while/body/eval_jaxpr/convert_element_type | solution.py:37
  119.9 1.1 gather_fusion.1
  121.3 1.1 gather_fusion
  124.4 9.4 %cosine_convert_fusion.2 = (bf16[2048,256]{1,0:T(8,128)(2,1)S(1)}, bf16[2048,256]{1,0:T(8,128)(2,1)S(1)}) fusion(s32[256]{0:T(256)S(1)} %iota_add_fusion.4, s32[2048]{0:T(1024)S(1)} %iota_add_fusion.5), kind=kLoop, calls=%fused_computation.19.clone.1 | loop fusion | flops 8912896 | bytes 2106368 | tf_op jit(solution)/shard_map/while/body/eval_jaxpr/convert_element_type | solution.py:37
  135.8 1.1 gather_fusion.1
  137.2 1.1 gather_fusion
  140.3 9.4 %cosine_convert_fusion.2 = (bf16[2048,256]{1,0:T(8,128)(2,1)S(1)}, bf16[2048,256]{1,0:T(8,128)(2,1)S(1)}) fusion(s32[256]{0:T(256)S(1)} %iota_add_fusion.4, s32[2048]{0:T(1024)S(1)} %iota_add_fusion.5), kind=kLoop, calls=%fused_computation.19.clone.1 | loop fusion | flops 8912896 | bytes 2106368 | tf_op jit(solution)/shard_map/while/body/eval_jaxpr/convert_element_type | solution.py:37
  151.7 1.1 gather_fusion.1
  153.1 1.1 gather_fusion
  156.2 9.4 %cosine_convert_fusion.2 = (bf16[2048,256]{1,0:T(8,128)(2,1)S(1)}, bf16[2048,256]{1,0:T(8,128)(2,1)S(1)}) fusion(s32[256]{0:T(256)S(1)} %iota_add_fusion.4, s32[2048]{0:T(1024)S(1)} %iota_add_fusion.5), kind=kLoop, calls=%fused_computation.19.clone.1 | loop fusion | flops 8912896 | bytes 2106368 | tf_op jit(solution)/shard_map/while/body/eval_jaxpr/convert_element_type | solution.py:37
  167.6 1.1 gather_fusion.1
  169.0 1.1 gather_fusion
  172.1 9.4 %cosine_convert_fusion.2 = (bf16[2048,256]{1,0:T(8,128)(2,1)S(1)}, bf16[2048,256]{1,0:T(8,128)(2,1)S(1)}) fusion(s32[256]{0:T(256)S(1)} %iota_add_fusion.4, s32[2048]{0:T(1024)S(1)} %iota_add_fusion.5), kind=kLoop, calls=%fused_computation.19.clone.1 | loop fusion | flops 8912896 | bytes 2106368 | tf_op jit(solution)/shard_map/while/body/eval_jaxpr/convert_element_type | solution.py:37
  183.5 1.1 gather_fusion.1
  184.9 1.1 gather_fusion
  188.0 9.4 %cosine_convert_fusion.2 = (bf16[2048,256]{1,0:T(8,128)(2,1)S(1)}, bf16[2048,256]{1,0:T(8,128)(2,1)S(1)}) fusion(s32[256]{0:T(256)S(1)} %iota_add_fusion.4, s32[2048]{0:T(1024)S(1)} %iota_add_fusion.5), kind=kLoop, calls=%fused_computation.19.clone.1 | loop fusion | flops 8912896 | bytes 2106368 | tf_op jit(solution)/shard_map/while/body/eval_jaxpr/convert_element_type | solution.py:37
  199.4 1.1 gather_fusion.1
  200.8 1.1 gather_fusion
  203.9 9.4 %cosine_convert_fusion.2 = (bf16[2048,256]{1,0:T(8,128)(2,1)S(1)}, bf16[2048,256]{1,0:T(8,128)(2,1)S(1)}) fusion(s32[256]{0:T(256)S(1)} %iota_add_fusion.4, s32[2048]{0:T(1024)S(1)} %iota_add_fusion.5), kind=kLoop, calls=%fused_computation.19.clone.1 | loop fusion | flops 8912896 | bytes 2106368 | tf_op jit(solution)/shard_map/while/body/eval_jaxpr/convert_element_type | solution.py:37
  215.3 1.1 gather_fusion.1
  216.7 1.1 gather_fusion
  219.8 9.4 %cosine_convert_fusion.2 = (bf16[2048,256]{1,0:T(8,128)(2,1)S(1)}, bf16[2048,256]{1,0:T(8,128)(2,1)S(1)}) fusion(s32[256]{0:T(256)S(1)} %iota_add_fusion.4, s32[2048]{0:T(1024)S(1)} %iota_add_fusion.5), kind=kLoop, calls=%fused_computation.19.clone.1 | loop fusion | flops 8912896 | bytes 2106368 | tf_op jit(solution)/shard_map/while/body/eval_jaxpr/convert_element_type | solution.py:37
  231.2 1.1 gather_fusion.1
  235.7 9.4 %cosine_convert_fusion.2 = (bf16[2048,256]{1,0:T(8,128)(2,1)S(1)}, bf16[2048,256]{1,0:T(8,128)(2,1)S(1)}) fusion(s32[256]{0:T(256)S(1)} %iota_add_fusion.4, s32[2048]{0:T(1024)S(1)} %iota_add_fusion.5), kind=kLoop, calls=%fused_computation.19.clone.1 | loop fusion | flops 8912896 | bytes 2106368 | tf_op jit(solution)/shard_map/while/body/eval_jaxpr/convert_element_type | solution.py:37
  251.6 9.4 %cosine_convert_fusion.2 = (bf16[2048,256]{1,0:T(8,128)(2,1)S(1)}, bf16[2048,256]{1,0:T(8,128)(2,1)S(1)}) fusion(s32[256]{0:T(256)S(1)} %iota_add_fusion.4, s32[2048]{0:T(1024)S(1)} %iota_add_fusion.5), kind=kLoop, calls=%fused_computation.19.clone.1 | loop fusion | flops 8912896 | bytes 2106368 | tf_op jit(solution)/shard_map/while/body/eval_jaxpr/convert_element_type | solution.py:37
  267.5 9.4 %cosine_convert_fusion.2 = (bf16[2048,256]{1,0:T(8,128)(2,1)S(1)}, bf16[2048,256]{1,0:T(8,128)(2,1)S(1)}) fusion(s32[256]{0:T(256)S(1)} %iota_add_fusion.4, s32[2048]{0:T(1024)S(1)} %iota_add_fusion.5), kind=kLoop, calls=%fused_computation.19.clone.1 | loop fusion | flops 8912896 | bytes 2106368 | tf_op jit(solution)/shard_map/while/body/eval_jaxpr/convert_element_type | solution.py:37
  283.4 9.4 %cosine_convert_fusion.2 = (bf16[2048,256]{1,0:T(8,128)(2,1)S(1)}, bf16[2048,256]{1,0:T(8,128)(2,1)S(1)}) fusion(s32[256]{0:T(256)S(1)} %iota_add_fusion.4, s32[2048]{0:T(1024)S(1)} %iota_add_fusion.5), kind=kLoop, calls=%fused_computation.19.clone.1 | loop fusion | flops 8912896 | bytes 2106368 | tf_op jit(solution)/shard_map/while/body/eval_jaxpr/convert_element_type | solution.py:37
  299.4 9.4 %cosine_convert_fusion.2 = (bf16[2048,256]{1,0:T(8,128)(2,1)S(1)}, bf16[2048,256]{1,0:T(8,128)(2,1)S(1)}) fusion(s32[256]{0:T(256)S(1)} %iota_add_fusion.4, s32[2048]{0:T(1024)S(1)} %iota_add_fusion.5), kind=kLoop, calls=%fused_computation.19.clone.1 | loop fusion | flops 8912896 | bytes 2106368 | tf_op jit(solution)/shard_map/while/body/eval_jaxpr/convert_element_type | solution.py:37
  310.5 24.4 %all-gather.3.cloned.1.call-done = f32[32,64,256]{2,1,0:T(8,128)} async-done(((f32[4,64,256]{2,1,0:T(8,128)}), f32[32,64,256]{2,1,0:T(8,128)}) %all-gather.3.cloned.1.call-update) | async-done | bytes 2097168 | tf_op jit(solution)/shard_map/all_gather | solution.py:13
  334.8 1.8 reduce_sum.49
  (302 shorter events, 80.6 us)
Async XLA Ops:
  6.5 1.4 copy-start
  6.5 328.3 %all-gather.3.cloned.1.call-start = ((), (), s32[]{:S(2)}) async-start(), calls=%async_computation | async-start | bytes 2359296 | tf_op jit(solution)/shard_map/all_gather | solution.py:13
  8.0 13.3 %copy-start.2 = (s32[63]{0:T(128)S(1)}, s32[63]{0:T(128)}, u32[]{:S(2)}) copy-start(s32[63]{0:T(128)} %param.11) | copy-start | bytes 760
  8.0 13.5 %copy-start.1 = (s32[63,2]{0,1:T(2,128)S(1)}, s32[63,2]{0,1:T(2,128)}, u32[]{:S(2)}) copy-start(s32[63,2]{0,1:T(2,128)} %param.10) | copy-start | bytes 1516
  11.6 30.1 %collective-permute-start.1 = (bf16[8,2,32768]{2,1,0:T(2,128)(2,1)S(1)}, bf16[8,2,32768]{2,1,0:T(2,128)(2,1)S(1)}, u32[]{:S(2)}, u32[]{:S(2)}) collective-permute-start(bf16[8,2,32768]{2,1,0:T(2,128)(2,1)S(1)} %broadcast_select_fusion.2), channel_id=1, source_target_pairs={{8,0},{16,8},{24,16},{32,24},{40,32},{48,40},{56,48},{64,56},{72,6... | collective-permute-start | bytes 3145736 | tf_op jit(solution)/shard_map/ppermute | solution.py:27
  19.3 28.7 %collective-permute-start = (bf16[8,2,32768]{2,1,0:T(2,128)(2,1)S(1)}, bf16[8,2,32768]{2,1,0:T(2,128)(2,1)}, u32[]{:S(2)}, u32[]{:S(2)}) collective-permute-start(bf16[8,2,32768]{2,1,0:T(2,128)(2,1)S(1)} %broadcast_select_fusion.2), channel_id=1, source_target_pairs={{0,8},{8,16},{16,24},{24,32},{32,40},{40,48},{48,56},{56,64},{64,7... | collective-permute-start | bytes 3145736 | tf_op jit(solution)/shard_map/ppermute | solution.py:24
Sparse Core Ops, SparseCore 0:
  310.6 24.1 all-gather.2
